TPU v7x, 512 devices: a whole 4x8x8 slice. The times are simulated.
512 devices in a mesh: dp: 64 (over z_hi, x, y), tensor: 8 (over z_lo, core).
Axes of the slice: x: 4, y: 8, z: 8 (z_hi: 2, z_lo: 4; z = z_hi * 4 + z_lo), core: 2. Of those that a mesh axis runs over, the one named last changes fastest.
Arguments:
- hidden_act: bfloat16 [24576, 36864], P('dp', 'tensor'), may hold values from -64 to 64
- out_grad: bfloat16 [24576, 4608], P('dp', 'tensor'), may hold values from -0.00012529303 to 0.00012529303
- privacy_noise: float32 [4608, 1024], P('dp', 'tensor'), may hold values from -4 to 4
Outputs:
- update: float32 [4608, 1024], P('dp', 'tensor')
- mean_sq_norm: float32 [], replicated
All inputs are finite; a program needn't handle non-finite values.
Results may differ from a plain program's by a relative error of at most 0.0003.
Values may be sent and summed in bfloat16 or wider, within the bound.
A program may use at most 64 MiB of HBM per device.

v0:
```python
import math

import jax
import jax.numpy as jnp
from jax import lax
from jax.sharding import PartitionSpec as P

D = 4608
FF = 36864
SEQ = 384
EX_DEV = 1
BLOCK = 128


def shards(hidden_act, out_grad, privacy_noise):
    examples = EX_DEV
    full_grad = lax.all_gather(out_grad, "tensor", axis=1, tiled=True)
    acts_each = hidden_act.reshape(examples, SEQ, hidden_act.shape[1])
    grads_each = full_grad.reshape(examples, SEQ, D)
    act_gram = jnp.einsum("esf,etf->est", acts_each, acts_each, preferred_element_type=jnp.float32)
    grad_gram = jnp.einsum(
        "esd,etd->est", grads_each, grads_each, preferred_element_type=jnp.float32
    )
    partial_value = jnp.sum(act_gram * grad_gram, axis=(1, 2))
    window_flat = hidden_act[:, :BLOCK]
    window = window_flat.reshape(examples, SEQ, BLOCK)
    dp_count = lax.axis_size("dp")
    batch = examples * dp_count
    scale = math.sqrt(FF * D / batch)
    own_rows = D // dp_count
    square_norm = lax.psum(partial_value, "tensor")
    factor = 1.0 / jnp.maximum(jnp.sqrt(square_norm), 1.0)
    total = lax.psum(jnp.sum(square_norm), "dp")
    columns = full_grad.reshape(examples, SEQ, own_rows * lax.axis_size("dp"))
    per_example = jnp.einsum("esd,esb->edb", columns, window, preferred_element_type=jnp.float32)
    summed = lax.psum_scatter(
        jnp.sum(factor[:, None, None] * per_example, axis=0), "dp", scatter_dimension=0, tiled=True
    )
    mean_sq_norm = total / batch
    update = scale * summed + privacy_noise
    return (update, mean_sq_norm)


def solution(mesh):
    return jax.shard_map(
        shards,
        mesh=mesh,
        in_specs=(P("dp", "tensor"), P("dp", "tensor"), P("dp", "tensor")),
        out_specs=(P("dp", "tensor"), P()),
        check_vma=False,
    )
```

profile of v0, /device:TPU:6, one launch (start us, length us, event | category | flops | bytes accessed | tf_op | source)
XLA Modules:
  0.0 941.0 jit_solution(8139933344849406870)
XLA Ops:
  7.2 0.0 all-gather.2.cloned.1.call-start
  7.2 0.7 all-gather.2.cloned.1.call-update
  7.9 0.0 reduce-scatter.4.cloned.1.call-start
  7.9 5.9 fusion.2
  13.8 52.5 %all-gather.2.cloned.1.call-done = bf16[384,4608]{0,1:T(8,128)(2,1)} async-done(((bf16[384,576]{0,1:T(8,128)(2,1)}), bf16[384,4608]{0,1:T(8,128)(2,1)}) %all-gather.2.cloned.1.call-update) | async-done | bytes 3538960 | tf_op jit(solution)/shard_map/all_gather | solution.py:17
  66.3 0.0 copy-start
  66.3 6.0 fusion
  72.3 15.1 %psum.14 = f32[1]{0:T(128)} all-reduce(f32[1]{0:T(128)} %bitcast), channel_id=1, replica_groups=mesh['dp'=64,'tensor'=8] {'tensor'}, use_global_device_ids=true, to_apply=%region_1.0 | all-reduce | flops 1 | bytes 8 | tf_op jit(solution)/shard_map/psum | solution.py:31
  88.2 0.0 copy-done
  88.2 3.4 convolution_multiply_fusion
  91.6 0.0 reduce-scatter.4.cloned.1.call-update
  91.6 188.5 %psum.15 = f32[]{:T(128)} all-reduce(f32[]{:T(128)} %bitcast.2), channel_id=1, replica_groups=mesh['dp'=64,'tensor'=8] {'dp'}, use_global_device_ids=true, to_apply=%region_3.0 | all-reduce | flops 1 | bytes 8 | tf_op jit(solution)/shard_map/psum | solution.py:33
  280.8 650.9 %reduce-scatter.4.cloned.1.call-done = f32[72,128]{1,0:T(8,128)} async-done(((f32[4608,128]{1,0:T(8,128)}), f32[72,128]{1,0:T(8,128)}) %reduce-scatter.4.cloned.1.call-update) | async-done | bytes 36880
  931.7 1.4 multiply_add_fusion
Async XLA Ops:
  7.2 59.2 %all-gather.2.cloned.1.call-start = ((), (), s32[]{:S(2)}) async-start(), calls=%async_computation.1 | async-start | bytes 3981312 | tf_op jit(solution)/shard_map/all_gather | solution.py:17
  7.9 923.8 %reduce-scatter.4.cloned.1.call-start = ((), (), s32[]{:S(2)}) async-start(), calls=%async_computation.2 | async-start | bytes 2396160
  66.3 21.8 %copy-start = (bf16[384,4608]{0,1:T(8,128)(2,1)S(1)}, bf16[384,4608]{0,1:T(8,128)(2,1)}, u32[]{:S(2)}) copy-start(bf16[384,4608]{0,1:T(8,128)(2,1)} %all-gather.2.cloned.1.call-done) | copy-start | bytes 10616836
Sparse Core Ops, SparseCore 0:
  10.1 56.2 all-gather.1
  91.7 839.8 reduce-scatter.3
where the time goes:
time: 941 us
  waiting for transfers between devices  704 us (75%)
  blocking collectives  204 us (22%)
  between operations  16.6 us (2%)
  matrix products  15.3 us (2%)
    unnamed x3, waiting for transfers between devices  652 us
    psum x1, blocking collectives, shards(): total = lax.psum(jnp.sum(square_norm), 'dp')  189 us
    all_gather x1, waiting for transfers between devices, shards(): full_grad = lax.all_gather(out_grad, 'tensor', axis=1, tiled=True)  52.5 us
  transfers between devices with their start and end apart: 2, of which 2 were waited for; matrix products, arithmetic and copies ran while one was open for 1% of the time, Pallas kernels for 0%

commit v1 on v0

v1 whole, which is shorter than its diff:
```python
import math

import jax
import jax.numpy as jnp
from jax import lax
from jax.experimental import pallas as pl
from jax.experimental.pallas import tpu as pltpu
from jax.sharding import PartitionSpec as P

D = 4608
FF = 36864
SEQ = 384
BLOCK = 128
BATCH = 64
OWN = D // 8
ROWS = D // 64
PIECE = ROWS + 8
CHUNKS = 3
SCALE = math.sqrt(FF * D / BATCH)
F32 = jnp.float32
MESH = pl.DeviceIdType.MESH


def ready_x(group):
    return lax.rem(3 * (group + 4), 5)


def group_of(x):
    return lax.rem(2 * x + 1, 5)


def kernel(
    h_hbm, g_ref, noise_ref, out_ref, mean_ref,
    h_ref, g_pair, win, a_half, gram_own, gram_in, s_in, x_out, x_own, x_in, sx_in, y_out, y_in,
    pair_recv, load_sem, send_sem, pair_sem, win_sem, gram_sem, s_sem, x_sem, sx_sem, y_sem,
):
    dp, t = lax.axis_index("dp"), lax.axis_index("tensor")
    zh, x, y = dp // 32, lax.rem(dp // 8, 4), lax.rem(dp, 8)
    zl, q = t // 2, lax.rem(t, 2)
    column = group_of(x)

    def device(zh_, x_, y_, zl_, q_):
        return (zh_ * 32 + x_ * 8 + y_, zl_ * 2 + q_)

    def peer_z(k):
        return device(zh, x, y, lax.rem(zl + k, 4), q)

    def peer_t(k):
        return (dp, lax.rem(t + k, 8))

    def peer_x(k):
        return device(zh, lax.rem(x + k, 4), y, zl, q)

    partner = (dp, t + 1 - 2 * q)
    sends = []

    def send(src, dst, recv, to):
        copy = pltpu.make_async_remote_copy(
            src_ref=src, dst_ref=dst, send_sem=send_sem.at[len(sends)], recv_sem=recv,
            device_id=to, device_id_type=MESH,
        )
        copy.start()
        sends.append(copy)

    def arrived(dst, recv):
        pltpu.make_async_copy(dst, dst, recv).wait()

    barrier = pltpu.get_barrier_semaphore()
    sources = [peer_t(k) for k in range(1, 8)] + [peer_x(k) for k in range(1, 4)]
    x_src = ready_x(zl)
    zl_src = zh * 2 + x // 2
    for k in range(16):
        sources.append(device(k // 8, x_src, k % 8, zl_src, q))
    for source in sources:
        pl.semaphore_signal(barrier, inc=1, device_id=source, device_id_type=MESH)

    part = h_ref.shape[1] // CHUNKS
    loads = []
    for c in range(CHUNKS):
        cut = pl.ds(c * part, part)
        loads.append(pltpu.make_async_copy(h_hbm.at[:, cut], h_ref.at[:, cut], load_sem.at[c]))
        loads[-1].start()
    loads[0].wait()
    win[zl] = h_ref[:, :BLOCK]
    pl.semaphore_wait(barrier, len(sources))

    send(g_ref, g_pair, pair_sem.at[0], partner)
    for k in range(1, 4):
        send(win.at[zl], win.at[zl], win_sem.at[zl], peer_z(k))

    gram = None
    for c in range(CHUNKS):
        if c:
            loads[c].wait()
        h = h_ref[:, c * part:(c + 1) * part]
        term = lax.dot_general(h, h, (((1,), (1,)), ((), ())), preferred_element_type=F32)
        gram = term if gram is None else gram + term
    blocks = [(0, 0), (0, 1), (0, 2), (1, 1), (1, 2), (2, 2)]

    def cut(matrix, b, p):
        i, j = blocks[b]
        return matrix[i * 128 + p * 32:i * 128 + (p + 1) * 32, j * 128:(j + 1) * 128]

    for b in range(6):
        for p in range(4):
            a_half[b // 3, p, b % 3] = cut(gram, b, p)
    send(a_half.at[1 - q], pair_recv, pair_sem.at[1], partner)

    arrived(g_pair, pair_sem.at[0])
    grad = None
    for ref in (g_ref, g_pair):
        g = ref[...]
        term = lax.dot_general(g, g, (((0,), (0,)), ((), ())), preferred_element_type=F32)
        grad = term if grad is None else grad + term
    for half in range(2):
        @pl.when(q == half)
        def _():
            for b in range(3):
                for p in range(4):
                    gram_own[p, 1, b] = cut(grad, half * 3 + b, p)

    arrived(pair_recv, pair_sem.at[1])
    gram_own[:, 0] = a_half[q] + pair_recv[...]
    for k in range(1, 4):
        to = lax.rem(zl + k, 4)
        send(gram_own.at[to], gram_in.at[k - 1], gram_sem.at[k - 1], peer_z(k))

    for k in range(1, 4):
        at = lax.rem(zl + k, 4)
        arrived(win.at[at], win_sem.at[at])
    for k in range(4):
        window = win[group_of(lax.rem(x + k, 4))]
        for side, ref in enumerate((g_ref, g_pair)):
            bucket = jnp.dot(ref[...], window, preferred_element_type=F32)
            if k:
                x_out[k - 1, side] = bucket
                send(x_out.at[k - 1, side], x_in.at[k - 1, side], x_sem.at[k - 1, side], peer_x(k))
            else:
                x_own[side] = bucket

    for k in range(1, 4):
        arrived(gram_in.at[k - 1], gram_sem.at[k - 1])
    total = gram_own[zl]
    for k in range(3):
        total = total + gram_in[k]
    both = total[0] * total[1]
    third = (2 - q).astype(F32)
    weighed = both[0] + 2.0 * both[1] + third * both[2]
    s_in[t] = jnp.full((8, 128), jnp.sum(weighed), F32)
    for k in range(1, 8):
        send(s_in.at[t], s_in.at[t], s_sem.at[t], peer_t(k))
    for k in range(1, 8):
        at = lax.rem(t + k, 8)
        arrived(s_in.at[at], s_sem.at[at])
    square = s_in[0]
    for k in range(1, 8):
        square = square + s_in[k]
    sx_in[x] = square
    for k in range(1, 4):
        send(sx_in.at[x], sx_in.at[x], sx_sem.at[x], peer_x(k))
    for k in range(1, 4):
        at = lax.rem(x + k, 4)
        arrived(sx_in.at[at], sx_sem.at[at])
    squares = sx_in[0] + sx_in[1] + sx_in[2] + sx_in[3]

    def factor(sq):
        return (1.0 / jnp.maximum(jnp.sqrt(sq), 1.0))[:1]

    own_factor = factor(sx_in[x])
    factors = [factor(sx_in[lax.rem(x + 4 - k, 4)]) for k in range(1, 4)]
    me = zh * 8 + y
    for side in range(2):
        for k in range(1, 4):
            arrived(x_in.at[k - 1, side], x_sem.at[k - 1, side])
        x_to = lax.rem(zl, 2) * 2 + (q if side == 0 else 1 - q)
        for r in range(8):
            rows = slice(r * ROWS, (r + 1) * ROWS)
            acc = own_factor * x_own[side, rows]
            for k in range(3):
                acc = acc + factors[k] * x_in[k, side, rows]
            y_out[side, r, :ROWS] = acc
            y_out[side, r, ROWS:] = squares
            send(y_out.at[side, r], y_in.at[me], y_sem.at[me], device(zl // 2, x_to, r, column, q))

    summed = None
    for k in range(16):
        arrived(y_in.at[k], y_sem.at[k])
        summed = y_in[k] if summed is None else summed + y_in[k]
    out_ref[...] = SCALE * summed[:ROWS] + noise_ref[...]
    mean_ref[...] = summed[ROWS:] / BATCH
    for copy in sends:
        copy.wait_send()


def shards(hidden_act, out_grad, privacy_noise):
    dma = pltpu.SemaphoreType.DMA
    vmem = pl.BlockSpec(memory_space=pltpu.VMEM)
    bf16 = jnp.bfloat16
    n_sends = 1 + 3 + 1 + 3 + 6 + 7 + 3 + 16
    update, mean = pl.pallas_call(
        kernel,
        out_shape=(jax.ShapeDtypeStruct((ROWS, BLOCK), F32), jax.ShapeDtypeStruct((8, 128), F32)),
        in_specs=[pl.BlockSpec(memory_space=pl.ANY), vmem, vmem],
        out_specs=(vmem, vmem),
        scratch_shapes=[
            pltpu.VMEM((SEQ, FF // 8), bf16),
            pltpu.VMEM((OWN, SEQ), bf16),
            pltpu.VMEM((4, SEQ, BLOCK), bf16),
            pltpu.VMEM((2, 4, 3, 32, 128), F32),
            pltpu.VMEM((4, 2, 3, 32, 128), F32),
            pltpu.VMEM((3, 2, 3, 32, 128), F32),
            pltpu.VMEM((8, 8, 128), F32),
            pltpu.VMEM((3, 2, OWN, BLOCK), F32),
            pltpu.VMEM((2, OWN, BLOCK), F32),
            pltpu.VMEM((3, 2, OWN, BLOCK), F32),
            pltpu.VMEM((4, 8, 128), F32),
            pltpu.VMEM((2, 8, PIECE, BLOCK), F32),
            pltpu.VMEM((16, PIECE, BLOCK), F32),
            pltpu.VMEM((4, 3, 32, 128), F32),
            dma((CHUNKS,)),
            dma((n_sends,)),
            dma((2,)),
            dma((4,)),
            dma((3,)),
            dma((8,)),
            dma((3, 2)),
            dma((4,)),
            dma((16,)),
        ],
        compiler_params=pltpu.CompilerParams(
            collective_id=0, has_side_effects=True, vmem_limit_bytes=40 * 2**20
        ),
        cost_estimate=pl.CostEstimate(flops=4 * 10**9, bytes_accessed=5 * 10**6, transcendentals=0),
    )(hidden_act, out_grad.T, privacy_noise)
    return (update, mean[0, 0])


def solution(mesh):
    return jax.shard_map(
        shards,
        mesh=mesh,
        in_specs=(P("dp", "tensor"), P("dp", "tensor"), P("dp", "tensor")),
        out_specs=(P("dp", "tensor"), P()),
        check_vma=False,
    )
```

time: 941 us -> 93.8 us (0.10)
  waiting for transfers between devices: 704 us -> 0 us
  blocking collectives: 204 us -> 0 us
  Pallas kernels: 0 us -> 86.7 us
  between operations: 16.6 us -> 0.65 us
  matrix products: 15.3 us -> 0 us
    unnamed x3 -> x0, waiting for transfers between devices: 652 us -> none
    psum x2 -> x0, blocking collectives: 204 us -> none  [the longest x1 189 us: shards(): total = lax.psum(jnp.sum(square_norm), 'dp')]
    pallas_call x0 -> x1, Pallas kernels: none -> 86.7 us  [shards(): pl.pallas_call(kernel, out_shape=(jax.ShapeDtypeStruct((ROWS, BLOCK), F32...]
    all_gather x1 -> x0, waiting for transfers between devices: 52.5 us -> none  [shards(): full_grad = lax.all_gather(out_grad, 'tensor', axis=1, tiled=True)]
    dot_general x3 -> x0, matrix products: 15.3 us -> none  [the longest x1 5.96 us: shards(): jnp.einsum('esd,etd->est', grads_each, grads_each, preferred_element_type...]
  transfers between devices with their start and end apart: 2 -> 0, of which waited for: 2 -> 0; matrix products, arithmetic and copies ran while one was open for 1% -> 0% of each run, Pallas kernels for 0% -> 0%
where the time goes in v1:
time: 93.8 us; the launch traced here: 92.2 us
  Pallas kernels  86.7 us (92%)
  local copies, waits for them, and re-layouts  4.9 us (5%)
    pallas_call x1, Pallas kernels, shards(): pl.pallas_call(kernel, out_shape=(jax.ShapeDtypeStruct((ROWS, BLOCK), F32...  86.7 us
    unnamed x7, local copies, waits for them, and re-layouts  4.39 us

profile of v1, /device:TPU:6, one launch (start us, length us, event | category | flops | bytes accessed | tf_op | source)
XLA Modules:
  0.0 92.2 jit_solution(18391523959497526387)
XLA Ops:
  0.6 0.0 copy-start
  0.6 2.0 %copy-done = bf16[384,4608]{1,0:T(8,128)(2,1)S(1)} copy-done((bf16[384,4608]{1,0:T(8,128)(2,1)S(1)}, bf16[384,4608]{1,0:T(8,128)(2,1)}, u32[]{:S(2)}) %copy-start) | copy-done | bytes 3538968
  2.6 0.0 copy-start.1
  2.6 1.0 %copy-done.1 = bf16[384,576]{0,1:T(8,128)(2,1)S(1)} copy-done((bf16[384,576]{0,1:T(8,128)(2,1)S(1)}, bf16[384,576]{0,1:T(8,128)(2,1)}, u32[]{:S(2)}) %copy-start.1) | copy-done | bytes 442392
  3.6 0.0 copy-start.2
  3.6 0.8 copy-done.2
  4.4 86.7 %shard_map.50 = (f32[72,128]{1,0:T(8,128)S(1)}, f32[8,128]{1,0:T(8,128)S(1)}) custom-call(bf16[384,4608]{1,0:T(8,128)(2,1)S(1)} %copy-done, bf16[576,384]{1,0:T(8,128)(2,1)S(1)} %bitcast.2, f32[72,128]{1,0:T(8,128)S(1)} %copy-done.2), custom_call_target="tpu_custom_call" | custom-call | flops 4000000000 | bytes 5000000 | tf_op jit(solution)/shard_map/pallas_call | solution.py:200
  91.1 0.5 slice.3
  91.6 0.6 copy.6
Async XLA Ops:
  0.6 2.0 %copy-start = (bf16[384,4608]{1,0:T(8,128)(2,1)S(1)}, bf16[384,4608]{1,0:T(8,128)(2,1)}, u32[]{:S(2)}) copy-start(bf16[384,4608]{1,0:T(8,128)(2,1)} %h_hbm.1) | copy-start | bytes 10616836
  2.6 1.0 %copy-start.1 = (bf16[384,576]{0,1:T(8,128)(2,1)S(1)}, bf16[384,576]{0,1:T(8,128)(2,1)}, u32[]{:S(2)}) copy-start(bf16[384,576]{0,1:T(8,128)(2,1)} %param.4) | copy-start | bytes 1327108
  3.6 0.8 copy-start.2

commit v2 on v1

v2 whole, which is shorter than its diff:
```python
import math

import jax
import jax.numpy as jnp
from jax import lax
from jax.experimental import pallas as pl
from jax.experimental.pallas import tpu as pltpu
from jax.sharding import PartitionSpec as P

D = 4608
FF = 36864
SEQ = 384
BLOCK = 128
BATCH = 64
OWN = D // 8
ROWS = D // 64
PIECE = ROWS + 8
CODED = OWN + 16
SHARE = 2 * ROWS + 16
SPAN = 86.0
STRIP = 96
CHUNKS = 3
SCALE = math.sqrt(FF * D / BATCH)
F32 = jnp.float32
MESH = pl.DeviceIdType.MESH


def ready_x(group):
    return lax.rem(3 * (group + 4), 5)


def group_of(x):
    return lax.rem(2 * x + 1, 5)


def scale_of(top):
    return (top * 1.01).astype(jnp.bfloat16).astype(F32)


def encode(value, inverse):
    root = jnp.sqrt(jnp.minimum(jnp.abs(value) * inverse, 1.0))
    code = jnp.exp(root * (2 * SPAN) - SPAN)
    return jnp.where(value < 0, -code, code).astype(jnp.bfloat16)


def decode(code, scale):
    code = code.astype(F32)
    root = jnp.log(jnp.abs(code)) * (0.5 / SPAN) + 0.5
    value = root * root * scale
    return jnp.where(code < 0, -value, value)


def inverse_of(scale):
    return 1.0 / jnp.maximum(scale, 1e-30)


def kernel(
    h_hbm, g_hbm, noise_hbm, out_ref, mean_ref,
    h_ref, g_ref, noise_ref, g_pair, win, a_half, gram_own, pair_recv, gram_in, s_in, bucket_ref, x_out, x_in, sx_in,
    acc_ref, y_out, y_in, p_out, p_in,
    load_sem, send_sem, x_send, pair_sem, win_sem, gram_sem, s_sem, x_sem, sx_sem, y_sem, p_sem,
):
    dp, t = lax.axis_index("dp"), lax.axis_index("tensor")
    zh, x, y = dp // 32, lax.rem(dp // 8, 4), lax.rem(dp, 8)
    zl, q = t // 2, lax.rem(t, 2)
    column = group_of(x)

    def device(zh_, x_, y_, zl_, q_):
        return (zh_ * 32 + x_ * 8 + y_, zl_ * 2 + q_)

    def peer_z(k):
        return device(zh, x, y, lax.rem(zl + k, 4), q)

    def peer_t(k):
        return (dp, lax.rem(t + k, 8))

    def peer_x(k):
        return device(zh, lax.rem(x + k, 4), y, zl, q)

    def peer_y(k):
        return device(zh, x, lax.rem(y + k, 8), zl, q)

    partner = (dp, t + 1 - 2 * q)
    sends = []

    def remote(src, dst, sent, recv, to):
        return pltpu.make_async_remote_copy(
            src_ref=src, dst_ref=dst, send_sem=sent, recv_sem=recv, device_id=to, device_id_type=MESH
        )

    def send(src, dst, recv, to):
        sends.append(remote(src, dst, send_sem.at[len(sends)], recv, to))
        sends[-1].start()

    def arrived(dst, recv):
        pltpu.make_async_copy(dst, dst, recv).wait()

    barrier = pltpu.get_barrier_semaphore()
    sources = [peer_t(k) for k in range(1, 8)] + [peer_x(k) for k in range(1, 4)] + [peer_y(k) for k in range(1, 8)]
    for k in range(2):
        sources.append(device(k, ready_x(zl), y, zh * 2 + x // 2, q))
    for source in sources:
        pl.semaphore_signal(barrier, inc=1, device_id=source, device_id_type=MESH)

    part = h_ref.shape[1] // CHUNKS
    loads = []

    def load(src, dst):
        loads.append(pltpu.make_async_copy(src, dst, load_sem.at[len(loads)]))
        loads[-1].start()

    for c in range(CHUNKS):
        load(h_hbm.at[:, pl.ds(c * part, part)], h_ref.at[:, pl.ds(c * part, part)])
        if c == 0:
            load(g_hbm, g_ref)
    load(noise_hbm, noise_ref)
    loads[0].wait()
    win[zl] = h_ref[:, :BLOCK]
    loads[1].wait()
    pl.semaphore_wait(barrier, len(sources))

    send(g_ref, g_pair, pair_sem.at[0], partner)
    for k in range(1, 4):
        send(win.at[zl], win.at[zl], win_sem.at[zl], peer_z(k))

    def share(j, side):
        group = lax.rem(zl + j, 4)
        owner = ready_x(group)
        bucket = jnp.dot((g_ref, g_pair)[side][...], win[group], preferred_element_type=F32)
        bucket_ref[j, side] = bucket
        scale = scale_of(jnp.max(jnp.abs(bucket)))
        inverse = inverse_of(scale)
        for row in range(0, OWN, STRIP):
            rows = slice(row, row + STRIP)
            x_out[j, side, rows] = encode(bucket_ref[j, side, rows], inverse)
        x_out[j, side, OWN:] = jnp.full((16, BLOCK), scale, F32).astype(jnp.bfloat16)
        copy = remote(
            x_out.at[j, side], x_in.at[x, side], x_send.at[j, side], x_sem.at[x, side], device(zh, owner, y, zl, q)
        )

        @pl.when(owner != x)
        def _():
            copy.start()
        return owner, copy

    shares = [share(0, 0)]

    gram = None
    for c in range(CHUNKS):
        if c:
            loads[c + 1].wait()
        h = h_ref[:, c * part:(c + 1) * part]
        term = lax.dot_general(h, h, (((1,), (1,)), ((), ())), preferred_element_type=F32)
        gram = term if gram is None else gram + term
    blocks = [(0, 0), (0, 1), (0, 2), (1, 1), (1, 2), (2, 2)]

    def cut(matrix, b, p):
        i, j = blocks[b]
        return matrix[i * 128 + p * 32:i * 128 + (p + 1) * 32, j * 128:(j + 1) * 128]

    for b in range(6):
        for p in range(4):
            a_half[b // 3, p, b % 3] = cut(gram, b, p)
    send(a_half.at[1 - q], pair_recv, pair_sem.at[1], partner)

    arrived(g_pair, pair_sem.at[0])
    grad = None
    for ref in (g_ref, g_pair):
        g = ref[...]
        term = lax.dot_general(g, g, (((0,), (0,)), ((), ())), preferred_element_type=F32)
        grad = term if grad is None else grad + term
    for half in range(2):
        @pl.when(q == half)
        def _():
            for b in range(3):
                for p in range(4):
                    gram_own[p, 1, b] = cut(grad, half * 3 + b, p)

    arrived(pair_recv, pair_sem.at[1])
    gram_own[:, 0] = a_half[q] + pair_recv[...]
    for k in range(1, 4):
        to = lax.rem(zl + k, 4)
        send(gram_own.at[to], gram_in.at[k - 1], gram_sem.at[k - 1], peer_z(k))

    shares.append(share(0, 1))
    for k in range(1, 4):
        at = lax.rem(zl + k, 4)
        arrived(win.at[at], win_sem.at[at])
        shares += [share(k, 0), share(k, 1)]

    for k in range(1, 4):
        arrived(gram_in.at[k - 1], gram_sem.at[k - 1])
    total = gram_own[zl]
    for k in range(3):
        total = total + gram_in[k]
    both = total[0] * total[1]
    third = (2 - q).astype(F32)
    weighed = both[0] + 2.0 * both[1] + third * both[2]
    s_in[t] = jnp.full((8, 128), jnp.sum(weighed), F32)
    for k in range(1, 8):
        send(s_in.at[t], s_in.at[t], s_sem.at[t], peer_t(k))
    for k in range(1, 8):
        at = lax.rem(t + k, 8)
        arrived(s_in.at[at], s_sem.at[at])
    square = s_in[0]
    for k in range(1, 8):
        square = square + s_in[k]
    sx_in[x] = square
    for k in range(1, 4):
        send(sx_in.at[x], sx_in.at[x], sx_sem.at[x], peer_x(k))
    for k in range(1, 4):
        at = lax.rem(x + k, 4)
        arrived(sx_in.at[at], sx_sem.at[at])
    squares = sx_in[0] + sx_in[1] + sx_in[2] + sx_in[3]

    def factor(sq):
        return (1.0 / jnp.maximum(jnp.sqrt(sq), 1.0))[:1]

    own = lax.rem(column - zl + 4, 4)
    own_factor = factor(sx_in[x])
    others = [lax.rem(x + k, 4) for k in range(1, 4)]
    factors = [factor(sx_in[at]) for at in others]
    for side in range(2):
        for at in others:
            arrived(x_in.at[at, side], x_sem.at[at, side])
        scales = [f * x_in[at, side, OWN:][:1].astype(F32) for f, at in zip(factors, others)]
        for row in range(0, OWN, STRIP):
            rows = slice(row, row + STRIP)
            acc = own_factor * bucket_ref[own, side, rows]
            for scale, at in zip(scales, others):
                acc = acc + decode(x_in[at, side, rows], scale)
            acc_ref[side, rows] = acc

    high = squares.astype(jnp.bfloat16).astype(F32)
    middle = (squares - high).astype(jnp.bfloat16).astype(F32)
    low = squares - high - middle
    line = lax.broadcasted_iota(jnp.int32, (8, 128), 0)
    top = jnp.max(jnp.abs(acc_ref[...]), axis=(0, 1))
    scale = scale_of(jnp.max(top))
    inverse = inverse_of(scale)
    head = jnp.where(line == 0, scale, jnp.where(line == 1, high, jnp.where(line == 2, middle, low)))
    tile = jnp.concatenate([head, head], axis=0).astype(jnp.bfloat16)
    for k in range(1, 8):
        to = lax.rem(y + k, 8)
        rows = pl.ds(pl.multiple_of(to * ROWS, 8), ROWS)
        both = jnp.concatenate([acc_ref[0, rows], acc_ref[1, rows]], axis=0)
        y_out[k - 1, :2 * ROWS] = encode(both, inverse)
        y_out[k - 1, 2 * ROWS:] = tile
        send(y_out.at[k - 1], y_in.at[y], y_sem.at[y], peer_y(k))
    rows = pl.ds(pl.multiple_of(y * ROWS, 8), ROWS)
    acc = jnp.concatenate([acc_ref[0, rows], acc_ref[1, rows]], axis=0)
    y_in[y, 2 * ROWS:] = tile
    for k in range(1, 8):
        at = lax.rem(y + k, 8)
        arrived(y_in.at[at], y_sem.at[at])
        scale = y_in[at, 2 * ROWS:].astype(F32)[:1]
        acc = acc + decode(y_in[at, :2 * ROWS], scale)
    squares = None
    for k in range(8):
        head = y_in[k, 2 * ROWS:].astype(F32)
        one = head[1:2] + head[2:3] + head[3:4]
        squares = one if squares is None else squares + one

    for side in range(2):
        x_to = lax.rem(zl, 2) * 2 + (q if side == 0 else 1 - q)
        p_out[side, :ROWS] = acc[side * ROWS:(side + 1) * ROWS]
        p_out[side, ROWS:] = jnp.broadcast_to(squares, (8, 128))
        send(p_out.at[side], p_in.at[zh], p_sem.at[zh], device(zl // 2, x_to, y, column, q))
    for k in range(2):
        arrived(p_in.at[k], p_sem.at[k])
    loads[-1].wait()
    summed = p_in[0] + p_in[1]
    out_ref[...] = SCALE * summed[:ROWS] + noise_ref[...]
    mean_ref[...] = summed[ROWS:ROWS + 1, :1] / BATCH
    for copy in sends:
        copy.wait_send()
    for owner, copy in shares:
        @pl.when(owner != x)
        def _():
            copy.wait_send()


def shards(hidden_act, out_grad, privacy_noise):
    dma = pltpu.SemaphoreType.DMA
    hbm = pl.BlockSpec(memory_space=pl.ANY)
    vmem = pl.BlockSpec(memory_space=pltpu.VMEM)
    bf16 = jnp.bfloat16
    n_sends = 1 + 3 + 1 + 3 + 7 + 3 + 7 + 2
    update, mean = pl.pallas_call(
        kernel,
        out_shape=(pltpu.VMEM((ROWS, BLOCK), F32), pltpu.VMEM((1, 1), F32)),
        in_specs=[hbm, hbm, hbm],
        out_specs=(vmem, vmem),
        scratch_shapes=[
            pltpu.VMEM((SEQ, FF // 8), bf16),
            pltpu.VMEM((OWN, SEQ), bf16),
            pltpu.VMEM((ROWS, BLOCK), F32),
            pltpu.VMEM((OWN, SEQ), bf16),
            pltpu.VMEM((4, SEQ, BLOCK), bf16),
            pltpu.VMEM((2, 4, 3, 32, 128), F32),
            pltpu.VMEM((4, 2, 3, 32, 128), F32),
            pltpu.VMEM((4, 3, 32, 128), F32),
            pltpu.VMEM((3, 2, 3, 32, 128), F32),
            pltpu.VMEM((8, 8, 128), F32),
            pltpu.VMEM((4, 2, OWN, BLOCK), F32),
            pltpu.VMEM((4, 2, CODED, BLOCK), bf16),
            pltpu.VMEM((4, 2, CODED, BLOCK), bf16),
            pltpu.VMEM((4, 8, 128), F32),
            pltpu.VMEM((2, OWN, BLOCK), F32),
            pltpu.VMEM((7, SHARE, BLOCK), bf16),
            pltpu.VMEM((8, SHARE, BLOCK), bf16),
            pltpu.VMEM((2, PIECE, BLOCK), F32),
            pltpu.VMEM((2, PIECE, BLOCK), F32),
            dma((CHUNKS + 2,)),
            dma((n_sends,)),
            dma((4, 2)),
            dma((2,)),
            dma((4,)),
            dma((3,)),
            dma((8,)),
            dma((4, 2)),
            dma((4,)),
            dma((8,)),
            dma((2,)),
        ],
        compiler_params=pltpu.CompilerParams(
            collective_id=0, has_side_effects=True, vmem_limit_bytes=60 * 2**20
        ),
        cost_estimate=pl.CostEstimate(flops=4 * 10**9, bytes_accessed=5 * 10**6, transcendentals=0),
    )(hidden_act, out_grad.T, privacy_noise)
    return (update, mean.reshape(()))


def solution(mesh):
    return jax.shard_map(
        shards,
        mesh=mesh,
        in_specs=(P("dp", "tensor"), P("dp", "tensor"), P("dp", "tensor")),
        out_specs=(P("dp", "tensor"), P()),
        check_vma=False,
    )
```

time: 93.8 us -> 63.6 us (0.68); the launches traced: 92.2 us -> 63.5 us
  Pallas kernels: 86.7 us -> 61.1 us
  local copies, waits for them, and re-layouts: 4.9 us -> 0.62 us
  between operations: 0.65 us -> 1.8 us
    pallas_call x1, Pallas kernels: 86.7 us -> 61.1 us  [shards(): pl.pallas_call(kernel, out_shape=(pltpu.VMEM((ROWS, BLOCK), F32), pltpu.V...]
    unnamed x7 -> x1, local copies, waits for them, and re-layouts: 4.39 us -> 0.62 us
where the time goes in v2:
time: 63.6 us; the launch traced here: 63.5 us
  Pallas kernels  61.1 us (96%)
  between operations  1.8 us (3%)
    pallas_call x1, Pallas kernels, shards(): pl.pallas_call(kernel, out_shape=(pltpu.VMEM((ROWS, BLOCK), F32), pltpu.V...  61.1 us

profile of v2, /device:TPU:6, one launch (start us, length us, event | category | flops | bytes accessed | tf_op | source)
XLA Modules:
  0.0 63.5 jit_solution(7136563626811802158)
XLA Ops:
  0.6 61.1 %shard_map.50 = (f32[72,128]{1,0:T(8,128)S(1)}, f32[1,1]{1,0:T(1,128)S(1)}) custom-call(bf16[384,4608]{1,0:T(8,128)(2,1)} %h_hbm.1, bf16[576,384]{1,0:T(8,128)(2,1)} %bitcast.2, f32[72,128]{1,0:T(8,128)} %noise_hbm.1), custom_call_target="tpu_custom_call" | custom-call | flops 4000000000 | bytes 5000000 | tf_op jit(solution)/shard_map/pallas_call | solution.py:289
  61.7 0.6 copy.7

commit v3 on v2

v3 whole, which is shorter than its diff:
```python
import math

import jax
import jax.numpy as jnp
from jax import lax
from jax.experimental import pallas as pl
from jax.experimental.pallas import tpu as pltpu
from jax.sharding import PartitionSpec as P

D = 4608
FF = 36864
SEQ = 384
BLOCK = 128
BATCH = 64
OWN = D // 8
ROWS = D // 64
PIECE = ROWS + 8
PAIR = 2 * ROWS
CODED = PAIR + 16
GRAM = 2 * 3 * 32
SPAN = 86.0
CHUNKS = 3
SCALE = math.sqrt(FF * D / BATCH)
F32 = jnp.float32
MESH = pl.DeviceIdType.MESH


def turn_of(group):
    return lax.rem(3 * (group + 4), 5)


def group_at(turn):
    return lax.rem(2 * turn + 1, 5)


def scale_of(value):
    top = jnp.max(jnp.max(jnp.abs(value), axis=0, keepdims=True), axis=1, keepdims=True)
    return (top * 1.01).astype(jnp.bfloat16).astype(F32)


def encode(value, inverse):
    root = jnp.sqrt(jnp.minimum(jnp.abs(value) * inverse, 1.0))
    code = jnp.exp(root * (2 * SPAN) - SPAN)
    return jnp.where(value < 0, -code, code)


def decode(code, scale):
    code = code.astype(F32)
    root = jnp.log(jnp.abs(code)) * (0.5 / SPAN) + 0.5
    value = root * root * scale
    return jnp.where(code < 0, -value, value)


def inverse_of(scale):
    return 1.0 / jnp.maximum(scale, 1e-30)


def pack(value, exact):
    scale = scale_of(value)
    high = exact.astype(jnp.bfloat16).astype(F32)
    middle = (exact - high).astype(jnp.bfloat16).astype(F32)
    low = exact - high - middle
    line = lax.broadcasted_iota(jnp.int32, (8, BLOCK), 0)
    head = jnp.where(line == 0, scale, jnp.where(line == 1, high, jnp.where(line == 2, middle, low)))
    return jnp.concatenate([encode(value, inverse_of(scale)), head], axis=0).astype(jnp.bfloat16)


def unpack(packed):
    packed = packed.astype(F32)
    rows = packed.shape[0] - 8
    head = packed[rows:]
    return decode(packed[:rows], head[:1]), head[1:2] + head[2:3] + head[3:4]


def kernel(
    h_hbm, g_hbm, noise_hbm, out_ref, mean_ref,
    h_ref, g_ref, noise_ref, g_pair, win, a_half, gram_own, pair_recv, gram_out, gram_in, s_in, bucket_ref, x_out, x_in,
    x_value, sx_in, s_line, acc_ref, y_out, y_in, p_out, p_in,
    load_sem, send_sem, x_send, p_send, pass_send, pair_sem, win_sem, gram_sem, s_sem, x_sem, sx_sem, y_sem, p_sem,
):
    dp, t = lax.axis_index("dp"), lax.axis_index("tensor")
    zh, x, y = dp // 32, lax.rem(dp // 8, 4), lax.rem(dp, 8)
    zl, q = t // 2, lax.rem(t, 2)
    column = group_at(lax.rem(x + 8 - y, 4))

    def device(zh_, x_, y_, zl_, q_):
        return (zh_ * 32 + x_ * 8 + y_, zl_ * 2 + q_)

    def peer_z(k):
        return device(zh, x, y, lax.rem(zl + k, 4), q)

    def peer_t(k):
        return (dp, lax.rem(t + k, 8))

    def peer_x(k):
        return device(zh, lax.rem(x + k, 4), y, zl, q)

    def peer_y(k):
        return device(zh, x, lax.rem(y + k, 8), zl, q)

    partner = (dp, t + 1 - 2 * q)
    sends = []

    def remote(src, dst, sent, recv, to):
        return pltpu.make_async_remote_copy(
            src_ref=src, dst_ref=dst, send_sem=sent, recv_sem=recv, device_id=to, device_id_type=MESH
        )

    def send(src, dst, recv, to):
        sends.append(remote(src, dst, send_sem.at[len(sends)], recv, to))
        sends[-1].start()

    def arrived(dst, recv):
        pltpu.make_async_copy(dst, dst, recv).wait()

    barrier = pltpu.get_barrier_semaphore()
    def greet(to):
        pl.semaphore_signal(barrier, inc=1, device_id=to, device_id_type=MESH)

    source_x, source_z = lax.rem(turn_of(zl) + y, 4), zh * 2 + x // 2
    for k in range(2):
        pl.when(~((k == zh) & (source_x == x) & (source_z == zl)))(lambda k=k: greet(device(k, source_x, y, source_z, q)))
    for to in [peer_y(k) for k in range(1, 8)] + [peer_t(k) for k in range(1, 8)] + [peer_x(k) for k in range(1, 4)]:
        greet(to)
    own_x = [lax.rem(zl, 2) * 2 + (q if side == 0 else 1 - q) for side in range(2)]
    stays = [(own_x[side] == x) & (zl // 2 == zh) & (column == zl) for side in range(2)]
    greeted = 17 + sum(1 - stay.astype(jnp.int32) for stay in stays)

    part = h_ref.shape[1] // CHUNKS
    loads = []

    def load(src, dst):
        loads.append(pltpu.make_async_copy(src, dst, load_sem.at[len(loads)]))
        loads[-1].start()

    for c in range(CHUNKS):
        load(h_hbm.at[:, pl.ds(c * part, part)], h_ref.at[:, pl.ds(c * part, part)])
        if c == 0:
            load(g_hbm, g_ref)
    load(noise_hbm, noise_ref)
    def grams(left, right, axis):
        def product(a, b):
            return lax.dot_general(a, b, (((axis,), (axis,)), ((), ())), preferred_element_type=F32)
        return product(left, right(slice(0, 256))), product(right(slice(256, 384)), right(slice(256, 384)))

    def act_term(c):
        columns = slice(c * part, (c + 1) * part)
        return grams(h_ref[:, columns], lambda rows: h_ref[rows, columns], 1)

    def plus(a, b):
        return tuple(i + j for i, j in zip(a, b))

    loads[0].wait()
    win[zl] = h_ref[:, :BLOCK]
    gram = act_term(0)
    for c in range(1, CHUNKS):
        loads[c + 1].wait()
        gram = plus(gram, act_term(c))
    loads[1].wait()
    blocks = [(0, 0), (1, 0), (2, 0), (1, 1), (2, 1), (2, 2)]

    def cut(matrices, b, p):
        i, j = blocks[b]
        if b == 5:
            return matrices[1][p * 32:(p + 1) * 32]
        return matrices[0][i * 128 + p * 32:i * 128 + (p + 1) * 32, j * 128:(j + 1) * 128]

    for b in range(6):
        for p in range(4):
            a_half[b // 3, p, b % 3] = cut(gram, b, p)
    pl.semaphore_wait(barrier, greeted)
    low = (zl < 2).astype(jnp.int32)
    near = [zl + 1 - 2 * lax.rem(zl, 2), 1 + low, 3 * low]

    def send_window(to):
        send(win.at[zl], win.at[zl], win_sem.at[zl], device(zh, x, y, to, q))

    middle = (zl == 1) | (zl == 2)
    send_window(near[0])
    send_window(near[1])

    def pass_window(of, to, n):
        copy = remote(win.at[of], win.at[of], pass_send.at[n], win_sem.at[of], device(zh, x, y, to, q))
        pl.when(middle)(copy.start)
        shares.append((middle, copy))

    shares = []
    pass_window(zl, near[2], 0)
    send(g_ref, g_pair, pair_sem.at[0], partner)
    send(a_half.at[1 - q], pair_recv, pair_sem.at[1], partner)

    def share(slot, side, group):
        bucket = jnp.dot((g_ref, g_pair)[side][...], win[group], preferred_element_type=F32)
        scale = scale_of(bucket)
        inverse = inverse_of(scale)
        tile = jnp.broadcast_to(scale, (16, BLOCK)).astype(jnp.bfloat16)
        for b in range(4):
            rows = slice(b * ROWS, (b + 1) * ROWS), slice((b + 4) * ROWS, (b + 5) * ROWS)
            value = jnp.concatenate([bucket[r] for r in rows], axis=0)
            bucket_ref[group, side, b] = value
            x_out[slot, side, b, :PAIR] = encode(value, inverse).astype(jnp.bfloat16)
            x_out[slot, side, b, PAIR:] = tile
        for k in (1, 3, 2):
            to = lax.rem(x + k, 4)
            b = lax.rem(to + 4 - turn_of(group), 4)
            copy = remote(
                x_out.at[slot, side, b], x_in.at[x, side, b], x_send.at[slot, side, k - 1], x_sem.at[x, side, b],
                device(zh, to, y, zl, q),
            )
            copy.start()
            shares.append((None, copy))

    arrived(g_pair, pair_sem.at[0])
    grad = plus(*(grams(ref[...], lambda rows: ref[:, rows], 0) for ref in (g_ref, g_pair)))
    for half in range(2):
        @pl.when(q == half)
        def _():
            for b in range(3):
                for p in range(4):
                    gram_own[p, 1, b] = cut(grad, half * 3 + b, p)
    share(0, 0, zl)

    arrived(pair_recv, pair_sem.at[1])
    gram_own[:, 0] = a_half[q] + pair_recv[...]
    tops = [scale_of(gram_own[:, i].reshape(4 * GRAM // 2, 128)) for i in range(2)]
    for k in range(1, 4):
        to = lax.rem(zl + k, 4)
        for i, top in enumerate(tops):
            code = encode(gram_own[to, i].reshape(GRAM // 2, 128), inverse_of(top))
            gram_out[k - 1, i * GRAM // 2:(i + 1) * GRAM // 2] = code.astype(jnp.bfloat16)
        line = lax.broadcasted_iota(jnp.int32, (16, 128), 0)
        gram_out[k - 1, GRAM:] = jnp.where(line < 8, tops[0], tops[1]).astype(jnp.bfloat16)
        send(gram_out.at[k - 1], gram_in.at[k - 1], gram_sem.at[k - 1], peer_z(k))

    share(0, 1, zl)

    def share_near(n):
        arrived(win.at[near[n]], win_sem.at[near[n]])
        if n == 2:
            pass_window(near[2], near[0], 1)
        for side in range(2):
            share(n + 1, side, near[n])

    share_near(0)
    share_near(1)
    share_near(2)

    for k in range(1, 4):
        arrived(gram_in.at[k - 1], gram_sem.at[k - 1])
    total = [gram_own[zl, i] for i in range(2)]
    for k in range(3):
        got = gram_in[k].astype(F32)
        for i in range(2):
            value = decode(got[i * GRAM // 2:(i + 1) * GRAM // 2], got[GRAM + 8 * i:GRAM + 8 * i + 1])
            total[i] = total[i] + value.reshape(3, 32, 128)
    both = total[0] * total[1]
    third = (2 - q).astype(F32)
    weighed = both[0] + 2.0 * both[1] + third * both[2]
    s_in[t] = jnp.full((8, 128), jnp.sum(weighed), F32)
    for k in range(1, 8):
        send(s_in.at[t], s_in.at[t], s_sem.at[t], peer_t(k))
    for k in range(1, 8):
        at = lax.rem(t + k, 8)
        arrived(s_in.at[at], s_sem.at[at])
    square = s_in[0]
    for k in range(1, 8):
        square = square + s_in[k]
    sx_in[x] = square
    for k in range(1, 4):
        send(sx_in.at[x], sx_in.at[x], sx_sem.at[x], peer_x(k))

    others = [lax.rem(x + k, 4) for k in range(1, 4)]

    def open_side(side):
        for k, at in enumerate(others):
            for b in range(4):
                arrived(x_in.at[at, side, b], x_sem.at[at, side, b])
                code = x_in[at, side, b].astype(F32)
                x_value[side, k, b] = decode(code[:PAIR], code[PAIR:PAIR + 1])

    def factor(sq):
        return (1.0 / jnp.maximum(jnp.sqrt(sq), 1.0))[:1]

    def add_side(side):
        for b in range(4):
            acc = own_factor * bucket_ref[group_at(lax.rem(x + 4 - b, 4)), side, b]
            for k in range(3):
                acc = acc + factors[k] * x_value[side, k, b]
            acc_ref[side, b * ROWS:(b + 1) * ROWS] = acc[:ROWS]
            acc_ref[side, (b + 4) * ROWS:(b + 5) * ROWS] = acc[ROWS:]
        for k in range(1, 8):
            rows = pl.ds(pl.multiple_of(lax.rem(y + k, 8) * ROWS, 8), ROWS)
            y_out[side, k - 1] = pack(acc_ref[side, rows], squares)
            send(y_out.at[side, k - 1], y_in.at[side, y], y_sem.at[side, y], peer_y(k))

    def to_owner(side):
        acc = acc_ref[side, pl.ds(pl.multiple_of(y * ROWS, 8), ROWS)]
        s_line[y] = jnp.broadcast_to(squares, (8, BLOCK))
        for k in range(1, 8):
            at = lax.rem(y + k, 8)
            arrived(y_in.at[side, at], y_sem.at[side, at])
            value, line = unpack(y_in[side, at])
            acc = acc + value
            s_line[at] = jnp.broadcast_to(line, (8, BLOCK))
        line = s_line[0]
        for k in range(1, 8):
            line = line + s_line[k]
        p_out[side] = pack(acc, line[:1])
        copy = remote(
            p_out.at[side], p_in.at[zh], p_send.at[side], p_sem.at[zh], device(zl // 2, own_x[side], y, column, q)
        )
        stay = pltpu.make_async_copy(p_out.at[side], p_in.at[zh], p_sem.at[zh])
        pl.when(stays[side])(stay.start)
        pl.when(~stays[side])(copy.start)
        shares.append((~stays[side], copy))

    open_side(0)
    for at in others:
        arrived(sx_in.at[at], sx_sem.at[at])
    squares = (sx_in[0] + sx_in[1] + sx_in[2] + sx_in[3])[:1]
    own_factor = factor(sx_in[x])
    factors = [factor(sx_in[at]) for at in others]
    add_side(0)
    open_side(1)
    add_side(1)
    to_owner(0)
    to_owner(1)
    summed = None
    for k in range(2):
        arrived(p_in.at[k], p_sem.at[k])
        got = unpack(p_in[k])
        summed = got if summed is None else plus(summed, got)
    loads[-1].wait()
    out_ref[...] = SCALE * summed[0] + noise_ref[...]
    mean_ref[...] = jnp.broadcast_to(summed[1] / BATCH, (8, BLOCK))
    for copy in sends:
        copy.wait_send()
    for wanted, copy in shares:
        if wanted is None:
            copy.wait_send()
        else:
            pl.when(wanted)(copy.wait_send)


def shards(hidden_act, out_grad, privacy_noise):
    dma = pltpu.SemaphoreType.DMA
    hbm = pl.BlockSpec(memory_space=pl.ANY)
    vmem = pl.BlockSpec(memory_space=pltpu.VMEM)
    bf16 = jnp.bfloat16
    n_sends = 1 + 2 + 1 + 3 + 7 + 3 + 14
    update, mean = pl.pallas_call(
        kernel,
        out_shape=(pltpu.VMEM((ROWS, BLOCK), F32), pltpu.VMEM((8, BLOCK), F32)),
        in_specs=[hbm, hbm, hbm],
        out_specs=(vmem, vmem),
        scratch_shapes=[
            pltpu.VMEM((SEQ, FF // 8), bf16),
            pltpu.VMEM((OWN, SEQ), bf16),
            pltpu.VMEM((ROWS, BLOCK), F32),
            pltpu.VMEM((OWN, SEQ), bf16),
            pltpu.VMEM((4, SEQ, BLOCK), bf16),
            pltpu.VMEM((2, 4, 3, 32, 128), F32),
            pltpu.VMEM((4, 2, 3, 32, 128), F32),
            pltpu.VMEM((4, 3, 32, 128), F32),
            pltpu.VMEM((3, GRAM + 16, 128), bf16),
            pltpu.VMEM((3, GRAM + 16, 128), bf16),
            pltpu.VMEM((8, 8, 128), F32),
            pltpu.VMEM((4, 2, 4, PAIR, BLOCK), F32),
            pltpu.VMEM((4, 2, 4, CODED, BLOCK), bf16),
            pltpu.VMEM((4, 2, 4, CODED, BLOCK), bf16),
            pltpu.VMEM((2, 3, 4, PAIR, BLOCK), F32),
            pltpu.VMEM((4, 8, 128), F32),
            pltpu.VMEM((8, 8, 128), F32),
            pltpu.VMEM((2, OWN, BLOCK), F32),
            pltpu.VMEM((2, 7, PIECE, BLOCK), bf16),
            pltpu.VMEM((2, 8, PIECE, BLOCK), bf16),
            pltpu.VMEM((2, PIECE, BLOCK), bf16),
            pltpu.VMEM((2, PIECE, BLOCK), bf16),
            dma((CHUNKS + 2,)),
            dma((n_sends,)),
            dma((4, 2, 4)),
            dma((2,)),
            dma((2,)),
            dma((2,)),
            dma((4,)),
            dma((3,)),
            dma((8,)),
            dma((4, 2, 4)),
            dma((4,)),
            dma((2, 8)),
            dma((2,)),
        ],
        compiler_params=pltpu.CompilerParams(
            collective_id=0, has_side_effects=True, vmem_limit_bytes=60 * 2**20
        ),
        cost_estimate=pl.CostEstimate(flops=4 * 10**9, bytes_accessed=5 * 10**6, transcendentals=0),
    )(hidden_act, out_grad.T, privacy_noise)
    return (update, mean[0, 0])


def solution(mesh):
    return jax.shard_map(
        shards,
        mesh=mesh,
        in_specs=(P("dp", "tensor"), P("dp", "tensor"), P("dp", "tensor")),
        out_specs=(P("dp", "tensor"), P()),
        check_vma=False,
    )
```

time: 63.6 us -> 56.1 us (0.88)
  the two profiles are of different devices: /device:TPU:6 before, /device:TPU:1 now
where the time goes in v3:
time: 56.1 us; the launch traced here: 56 us
  Pallas kernels  54.2 us (97%)
  local copies, waits for them, and re-layouts  1.13 us (2%)
  between operations  0.64 us (1%)
    pallas_call x1, Pallas kernels, shards(): pl.pallas_call(kernel, out_shape=(pltpu.VMEM((ROWS, BLOCK), F32), pltpu.V...  54.2 us

profile of v3, /device:TPU:1, one launch (start us, length us, event | category | flops | bytes accessed | tf_op | source)
XLA Modules:
  0.0 56.0 jit_solution(2618307677812767912)
XLA Ops:
  0.6 54.2 %shard_map.50 = (f32[72,128]{1,0:T(8,128)S(1)}, f32[8,128]{1,0:T(8,128)S(1)}) custom-call(bf16[384,4608]{1,0:T(8,128)(2,1)} %h_hbm.1, bf16[576,384]{1,0:T(8,128)(2,1)} %bitcast.2, f32[72,128]{1,0:T(8,128)} %noise_hbm.1), custom_call_target="tpu_custom_call" | custom-call | flops 4000000000 | bytes 5000000 | tf_op jit(solution)/shard_map/pallas_call | solution.py:351
  54.8 0.5 slice.3
  55.4 0.6 %copy.6 = f32[72,128]{1,0:T(8,128)} copy(f32[72,128]{1,0:T(8,128)S(1)} %get-tuple-element.6) | data formatting | bytes 73728

commit v4 on v3

--- a/solution.py
+++ b/solution.py
@@ -157,6 +157,7 @@
         loads[c + 1].wait()
         gram = plus(gram, act_term(c))
     loads[1].wait()
+    grad = grams(g_ref[...], lambda rows: g_ref[:, rows], 0)
     blocks = [(0, 0), (1, 0), (2, 0), (1, 1), (2, 1), (2, 2)]
 
     def cut(matrices, b, p):
@@ -167,7 +168,8 @@
 
     for b in range(6):
         for p in range(4):
-            a_half[b // 3, p, b % 3] = cut(gram, b, p)
+            a_half[b // 3, p, 0, b % 3] = cut(gram, b, p)
+            a_half[b // 3, p, 1, b % 3] = cut(grad, b, p)
     pl.semaphore_wait(barrier, greeted)
     low = (zl < 2).astype(jnp.int32)
     near = [zl + 1 - 2 * lax.rem(zl, 2), 1 + low, 3 * low]
@@ -186,8 +188,8 @@
 
     shares = []
     pass_window(zl, near[2], 0)
+    send(a_half.at[1 - q], pair_recv, pair_sem.at[1], partner)
     send(g_ref, g_pair, pair_sem.at[0], partner)
-    send(a_half.at[1 - q], pair_recv, pair_sem.at[1], partner)
 
     def share(slot, side, group):
         bucket = jnp.dot((g_ref, g_pair)[side][...], win[group], preferred_element_type=F32)
@@ -210,18 +212,9 @@
             copy.start()
             shares.append((None, copy))
 
-    arrived(g_pair, pair_sem.at[0])
-    grad = plus(*(grams(ref[...], lambda rows: ref[:, rows], 0) for ref in (g_ref, g_pair)))
-    for half in range(2):
-        @pl.when(q == half)
-        def _():
-            for b in range(3):
-                for p in range(4):
-                    gram_own[p, 1, b] = cut(grad, half * 3 + b, p)
     share(0, 0, zl)
-
     arrived(pair_recv, pair_sem.at[1])
-    gram_own[:, 0] = a_half[q] + pair_recv[...]
+    gram_own[...] = a_half[q] + pair_recv[...]
     tops = [scale_of(gram_own[:, i].reshape(4 * GRAM // 2, 128)) for i in range(2)]
     for k in range(1, 4):
         to = lax.rem(zl + k, 4)
@@ -232,18 +225,22 @@
         gram_out[k - 1, GRAM:] = jnp.where(line < 8, tops[0], tops[1]).astype(jnp.bfloat16)
         send(gram_out.at[k - 1], gram_in.at[k - 1], gram_sem.at[k - 1], peer_z(k))
 
+    arrived(g_pair, pair_sem.at[0])
     share(0, 1, zl)
 
+    def window_arrived(n):
+        arrived(win.at[near[n]], win_sem.at[near[n]])
+
     def share_near(n):
-        arrived(win.at[near[n]], win_sem.at[near[n]])
-        if n == 2:
-            pass_window(near[2], near[0], 1)
         for side in range(2):
             share(n + 1, side, near[n])
 
+    window_arrived(0)
     share_near(0)
+    window_arrived(1)
     share_near(1)
-    share_near(2)
+    pl.when(middle)(lambda: window_arrived(2))
+    pass_window(near[2], near[0], 1)
 
     for k in range(1, 4):
         arrived(gram_in.at[k - 1], gram_sem.at[k - 1])
@@ -259,6 +256,8 @@
     s_in[t] = jnp.full((8, 128), jnp.sum(weighed), F32)
     for k in range(1, 8):
         send(s_in.at[t], s_in.at[t], s_sem.at[t], peer_t(k))
+    pl.when(~middle)(lambda: window_arrived(2))
+    share_near(2)
     for k in range(1, 8):
         at = lax.rem(t + k, 8)
         arrived(s_in.at[at], s_sem.at[at])
@@ -288,7 +287,7 @@
                 acc = acc + factors[k] * x_value[side, k, b]
             acc_ref[side, b * ROWS:(b + 1) * ROWS] = acc[:ROWS]
             acc_ref[side, (b + 4) * ROWS:(b + 5) * ROWS] = acc[ROWS:]
-        for k in range(1, 8):
+        for k in (4, 3, 5, 2, 6, 1, 7):
             rows = pl.ds(pl.multiple_of(lax.rem(y + k, 8) * ROWS, 8), ROWS)
             y_out[side, k - 1] = pack(acc_ref[side, rows], squares)
             send(y_out.at[side, k - 1], y_in.at[side, y], y_sem.at[side, y], peer_y(k))
@@ -359,9 +358,9 @@
             pltpu.VMEM((ROWS, BLOCK), F32),
             pltpu.VMEM((OWN, SEQ), bf16),
             pltpu.VMEM((4, SEQ, BLOCK), bf16),
-            pltpu.VMEM((2, 4, 3, 32, 128), F32),
+            pltpu.VMEM((2, 4, 2, 3, 32, 128), F32),
             pltpu.VMEM((4, 2, 3, 32, 128), F32),
-            pltpu.VMEM((4, 3, 32, 128), F32),
+            pltpu.VMEM((4, 2, 3, 32, 128), F32),
             pltpu.VMEM((3, GRAM + 16, 128), bf16),
             pltpu.VMEM((3, GRAM + 16, 128), bf16),
             pltpu.VMEM((8, 8, 128), F32),

time: 56.1 us -> 53.6 us (0.955)
  the two profiles are of different devices: /device:TPU:1 before, /device:TPU:2 now
where the time goes in v4:
time: 53.6 us; the launch traced here: 53.4 us
  Pallas kernels  51.7 us (96%)
  local copies, waits for them, and re-layouts  1.13 us (2%)
  between operations  0.64 us (1%)
    pallas_call x1, Pallas kernels, shards(): pl.pallas_call(kernel, out_shape=(pltpu.VMEM((ROWS, BLOCK), F32), pltpu.V...  51.7 us

profile of v4, /device:TPU:2, one launch (start us, length us, event | category | flops | bytes accessed | tf_op | source)
XLA Modules:
  0.0 53.4 jit_solution(18167265096477050765)
XLA Ops:
  0.6 51.7 %shard_map.50 = (f32[72,128]{1,0:T(8,128)S(1)}, f32[8,128]{1,0:T(8,128)S(1)}) custom-call(bf16[384,4608]{1,0:T(8,128)(2,1)} %h_hbm.1, bf16[576,384]{1,0:T(8,128)(2,1)} %bitcast.2, f32[72,128]{1,0:T(8,128)} %noise_hbm.1), custom_call_target="tpu_custom_call" | custom-call | flops 4000000000 | bytes 5000000 | tf_op jit(solution)/shard_map/pallas_call | solution.py:350
  52.3 0.5 slice.3
  52.8 0.6 %copy.6 = f32[72,128]{1,0:T(8,128)} copy(f32[72,128]{1,0:T(8,128)S(1)} %get-tuple-element.6) | data formatting | bytes 73728

commit v5 on v4

--- a/solution.py
+++ b/solution.py
@@ -153,6 +153,24 @@
     loads[0].wait()
     win[zl] = h_ref[:, :BLOCK]
     gram = act_term(0)
+    pl.semaphore_wait(barrier, greeted)
+    low = (zl < 2).astype(jnp.int32)
+    near = [zl + 1 - 2 * lax.rem(zl, 2), 1 + low, 3 * low]
+
+    def send_window(to):
+        send(win.at[zl], win.at[zl], win_sem.at[zl], device(zh, x, y, to, q))
+
+    middle = (zl == 1) | (zl == 2)
+    send_window(near[0])
+    send_window(near[1])
+
+    def pass_window(of, to, n):
+        copy = remote(win.at[of], win.at[of], pass_send.at[n], win_sem.at[of], device(zh, x, y, to, q))
+        pl.when(middle)(copy.start)
+        shares.append((middle, copy))
+
+    shares = []
+    pass_window(zl, near[2], 0)
     for c in range(1, CHUNKS):
         loads[c + 1].wait()
         gram = plus(gram, act_term(c))
@@ -170,24 +188,6 @@
         for p in range(4):
             a_half[b // 3, p, 0, b % 3] = cut(gram, b, p)
             a_half[b // 3, p, 1, b % 3] = cut(grad, b, p)
-    pl.semaphore_wait(barrier, greeted)
-    low = (zl < 2).astype(jnp.int32)
-    near = [zl + 1 - 2 * lax.rem(zl, 2), 1 + low, 3 * low]
-
-    def send_window(to):
-        send(win.at[zl], win.at[zl], win_sem.at[zl], device(zh, x, y, to, q))
-
-    middle = (zl == 1) | (zl == 2)
-    send_window(near[0])
-    send_window(near[1])
-
-    def pass_window(of, to, n):
-        copy = remote(win.at[of], win.at[of], pass_send.at[n], win_sem.at[of], device(zh, x, y, to, q))
-        pl.when(middle)(copy.start)
-        shares.append((middle, copy))
-
-    shares = []
-    pass_window(zl, near[2], 0)
     send(a_half.at[1 - q], pair_recv, pair_sem.at[1], partner)
     send(g_ref, g_pair, pair_sem.at[0], partner)
 

time: 53.6 us -> 51.9 us (0.968)
  the two profiles are of different devices: /device:TPU:2 before, /device:TPU:1 now
where the time goes in v5:
time: 51.9 us; the launch traced here: 51.8 us
  Pallas kernels  50 us (96%)
  local copies, waits for them, and re-layouts  1.13 us (2%)
  between operations  0.64 us (1%)
    pallas_call x1, Pallas kernels, shards(): pl.pallas_call(kernel, out_shape=(pltpu.VMEM((ROWS, BLOCK), F32), pltpu.V...  50 us

profile of v5, /device:TPU:1, one launch (start us, length us, event | category | flops | bytes accessed | tf_op | source)
XLA Modules:
  0.0 51.8 jit_solution(4574000165724634529)
XLA Ops:
  0.6 50.0 %shard_map.50 = (f32[72,128]{1,0:T(8,128)S(1)}, f32[8,128]{1,0:T(8,128)S(1)}) custom-call(bf16[384,4608]{1,0:T(8,128)(2,1)} %h_hbm.1, bf16[576,384]{1,0:T(8,128)(2,1)} %bitcast.2, f32[72,128]{1,0:T(8,128)} %noise_hbm.1), custom_call_target="tpu_custom_call" | custom-call | flops 4000000000 | bytes 5000000 | tf_op jit(solution)/shard_map/pallas_call | solution.py:350
  50.6 0.5 slice.3
  51.1 0.6 %copy.6 = f32[72,128]{1,0:T(8,128)} copy(f32[72,128]{1,0:T(8,128)S(1)} %get-tuple-element.6) | data formatting | bytes 73728
